TPU v7x, 512 devices: a whole 4x8x8 slice. The times are simulated.
512 devices in a mesh: band: 16 (over z, core), tile: 32 (over y, x).
Axes of the slice: x: 4, y: 8, z: 8, core: 2. Of those that a mesh axis runs over, the one named last changes fastest.
Arguments:
- sources: bfloat16 [524288, 256], P(('band', 'tile')), may hold values from -6 to 6
- observed: bfloat16 [8192, 256], P('tile'), may hold values from -6 to 6
- v_factors: bfloat16 [8, 96, 524288], P(None, None, ('band', 'tile')), may hold values from -0.1875 to 0.1875
- u_factors: bfloat16 [512, 96, 8192], P('band', None, 'tile'), may hold values from -0.03125 to 0.03125
- tile_ranks: int32 [8, 512], P(None, ('band', 'tile')), may hold values from 32 to 96
- v_exponents: int32 [8, 512], P(None, ('band', 'tile')), may hold values from -1 to 1
- u_exponents: int32 [8, 512], P(None, ('band', 'tile')), may hold values from -1 to 1
Outputs:
- residual: float32 [8192, 256], P('tile', 'band')
- gradient: bfloat16 [524288, 256], P(('band', 'tile'))
All inputs are finite; a program needn't handle non-finite values.
Results may differ from a plain program's by a relative error of at most 0.012.
Values may be sent and summed in bfloat16 or wider, within the bound.
A program may use at most 64 MiB of HBM per device.

v0:
```python
import jax
import jax.numpy as jnp
from jax import lax
from jax.sharding import PartitionSpec as P


def local(sources, observed, v_factors, u_factors, tile_ranks, v_exponents, u_exponents):
    tile_count = lax.axis_size("tile")
    band_count = lax.axis_size("band")
    row_tiles = v_factors.shape[0]
    rank_max = v_factors.shape[1]
    slices_per = tile_count // row_tiles
    rank_index = jnp.arange(rank_max, dtype=jnp.int32)
    weight = (rank_index[None, :] < tile_ranks).astype(jnp.float32)
    weight = weight * jnp.exp2((v_exponents + u_exponents).astype(jnp.float32))
    products = jnp.einsum("ikb,bs->iks", v_factors, sources, preferred_element_type=jnp.float32)
    pieces = (products * weight[:, :, None]).astype(jnp.bfloat16)
    outgoing = jnp.repeat(pieces, slices_per, axis=0)
    incoming = lax.all_to_all(outgoing, "tile", split_axis=0, concat_axis=0, tiled=True)
    partial_value = jnp.einsum(
        "ukh,uks->hs", u_factors, incoming, preferred_element_type=jnp.float32
    )
    col_width = observed.shape[1] // band_count
    offset = lax.axis_index("band") * col_width
    totals = lax.psum(partial_value, "band")
    full_rows = totals - observed.astype(jnp.float32)
    residual = lax.dynamic_slice_in_dim(full_rows, offset, col_width, 1)
    residual_rows = full_rows.astype(jnp.bfloat16)
    adjoint_part = jnp.einsum(
        "ukh,hs->uks", u_factors, residual_rows, preferred_element_type=jnp.float32
    )
    returned = lax.all_to_all(
        adjoint_part.astype(jnp.bfloat16), "tile", split_axis=0, concat_axis=0, tiled=True
    )
    summed = (
        returned.astype(jnp.float32)
        .reshape(row_tiles, slices_per, rank_max, returned.shape[2])
        .sum(axis=1)
    )
    adjoint = (summed * weight[:, :, None]).astype(jnp.bfloat16)
    gradient = jnp.einsum("ikb,iks->bs", v_factors, adjoint, preferred_element_type=jnp.float32)
    return (residual, gradient.astype(jnp.bfloat16))


def solution(mesh):
    in_specs = (
        P(("band", "tile"), None),
        P("tile", None),
        P(None, None, ("band", "tile")),
        P("band", None, "tile"),
        P(None, ("band", "tile")),
        P(None, ("band", "tile")),
        P(None, ("band", "tile")),
    )
    out_specs = (P("tile", "band"), P(("band", "tile"), None))
    return jax.shard_map(local, mesh=mesh, in_specs=in_specs, out_specs=out_specs, check_vma=False)
```

profile of v0, /device:TPU:6, one launch (start us, length us, event | category | flops | bytes accessed | tf_op | source)
XLA Modules:
  0.0 238.2 jit_solution(13547615035790127038)
XLA Ops:
  7.2 0.0 copy-start
  7.2 0.0 all-reduce.2.cloned.1.call-start
  7.2 0.8 exponential_bitcast_fusion
  8.0 0.7 fusion.8
  8.7 2.1 fusion.2
  10.8 0.2 broadcast_in_dim.2
  11.0 49.3 %all_to_all.10 = bf16[32,96,256]{2,1,0:T(8,128)(2,1)S(1)} all-to-all(bf16[32,96,256]{2,1,0:T(8,128)(2,1)S(1)} %bitcast.32), channel_id=1, replica_groups=mesh['band'=16,'tile'=32] {'tile'}, dimensions={0} | all-to-all | bytes 3145728 | tf_op jit(solution)/shard_map/all_to_all | solution.py:19
  60.3 0.0 copy-done
  60.3 0.0 copy-start.1
  60.3 1.3 convolution_bitcast_fusion.1
  61.6 0.0 all-reduce.2.cloned.1.call-update
  61.7 0.0 copy-done.1
  61.7 0.1 copy.9
  61.8 114.6 %all-reduce.2.cloned.1.call-done = f32[256,256]{0,1:T(8,128)} async-done(((f32[256,256]{0,1:T(8,128)}), f32[256,256]{0,1:T(8,128)}) %all-reduce.2.cloned.1.call-update) | async-done | bytes 262160 | tf_op jit(solution)/shard_map/psum | solution.py:25
  176.3 1.0 convert_subtract_fusion
  177.3 1.8 fusion
  179.1 9.9 %all-to-all-start.1 = ((bf16[32,96,256]{2,1,0:T(8,128)(2,1)}), bf16[32,96,256]{2,1,0:T(8,128)(2,1)S(1)}, u32[]{:S(2)}, u32[]{:S(2)}) async-start(bf16[32,96,256]{2,1,0:T(8,128)(2,1)} %fusion), calls=%async_computation.1 | async-start | bytes 3145728 | tf_op jit(solution)/shard_map/all_to_all | solution.py:32
  188.9 0.6 constant_dynamic-slice_fusion
  189.6 38.7 %all-to-all-done.1 = bf16[32,96,256]{2,1,0:T(8,128)(2,1)S(1)} async-done(((bf16[32,96,256]{2,1,0:T(8,128)(2,1)}), bf16[32,96,256]{2,1,0:T(8,128)(2,1)S(1)}, u32[]{:S(2)}, u32[]{:S(2)}) %all-to-all-start.1) | async-done | bytes 1572896 | tf_op jit(solution)/shard_map/all_to_all | solution.py:32
  228.3 0.0 copy-start.2
  228.3 0.2 convert_reduce_fusion
  228.5 1.2 copy-done.2
  229.7 0.7 fusion.3
  230.4 1.0 copy.11
Async XLA Ops:
  7.2 53.2 %copy-start = (bf16[32,96,256]{2,1,0:T(8,128)(2,1)S(1)}, bf16[32,96,256]{2,1,0:T(8,128)(2,1)}, u32[]{:S(2)}) copy-start(bf16[32,96,256]{2,1,0:T(8,128)(2,1)} %param.10) | copy-start | bytes 4718596
  7.2 169.1 %all-reduce.2.cloned.1.call-start = ((), (), s32[]{:S(2)}) async-start(), calls=%async_computation.2 | async-start | bytes 524288 | tf_op jit(solution)/shard_map/psum | solution.py:25
  60.3 1.3 copy-start.1
  179.1 49.2 %all-to-all-start.1 = ((bf16[32,96,256]{2,1,0:T(8,128)(2,1)}), bf16[32,96,256]{2,1,0:T(8,128)(2,1)S(1)}, u32[]{:S(2)}, u32[]{:S(2)}) async-start(bf16[32,96,256]{2,1,0:T(8,128)(2,1)} %fusion), calls=%async_computation.1 | async-start | bytes 3145728 | tf_op jit(solution)/shard_map/all_to_all | solution.py:32
  228.3 1.4 copy-start.2
Sparse Core Ops, SparseCore 0:
  61.8 114.5 all-reduce.1
where the time goes:
time: 239 us; the launch traced here: 238 us
  waiting for transfers between devices  153 us (64%)
  blocking collectives  49.3 us (21%)
  between operations  14.1 us (6%)
  starting transfers between devices  9.89 us (4%)
  matrix products  5.88 us (2%)
  local copies, waits for them, and re-layouts  3.08 us (1%)
  other arithmetic  2.71 us (1%)
    psum x1, waiting for transfers between devices, local(): totals = lax.psum(partial_value, 'band')  115 us
    all_to_all x1, blocking collectives, local(): lax.all_to_all(outgoing, 'tile', split_axis=0, concat_axis=0, tiled=True)  49.3 us
    all_to_all x1, waiting for transfers between devices, local(): lax.all_to_all(adjoint_part.astype(jnp.bfloat16), 'tile', split_axis=0, c...  38.7 us
    all_to_all x1, starting transfers between devices, local(): lax.all_to_all(adjoint_part.astype(jnp.bfloat16), 'tile', split_axis=0, c...  9.85 us
  transfers between devices with their start and end apart: 2, of which 2 were waited for; matrix products, arithmetic and copies ran while one was open for 0% of the time, Pallas kernels for 0%

commit v1 on v0

v1 whole, which is shorter than its diff:
```python
import functools

import jax
import jax.numpy as jnp
from jax import lax
from jax.experimental import pallas as pl
from jax.experimental.pallas import tpu as pltpu
from jax.sharding import PartitionSpec as P

NX = 4
NH = 1
LAG = 2
F32, BF16 = jnp.float32, jnp.bfloat16
AR_TYPE = jnp.bfloat16


def displacements(ny):
    order = [0]
    for step in range(1, ny // 2 + 1):
        order.append(step)
        if ny - step != step:
            order.append(ny - step)
    return order


def dot(a, b):
    return jnp.dot(a, b, preferred_element_type=F32)


def kernel(
    ny, nb,
    src_hbm, obs_hbm, v_hbm, u_hbm, rank_ref, vexp_ref, uexp_ref,
    res_out, grad_out,
    src, obs, v, u, ut, vt, inc, out, acc,
    ar_out, ar_in, ag_out, ag_in, rows, res_t,
    part, via, comb, from_l, from_r, ys, ret, adj,
    load_sem, ysend, yrecv, xsend, xrecv, arsend, arrecv, agsend, agrecv, bsend, brecv, zsend, zrecv,
):
    tile = lax.axis_index("tile")
    band = lax.axis_index("band")
    y, x = tile // NX, tile % NX
    order = displacements(ny)
    rmax = v.shape[1]
    width = inc.shape[-1]
    rb = ar_out.shape[2]

    def mod(value, n):
        return lax.rem(value + n, n)

    xr, xl, xf = mod(x + 1, NX), mod(x - 1, NX), mod(x + 2, NX)
    right, left = {"tile": y * NX + xr}, {"tile": y * NX + xl}
    rows_to = [{"tile": mod(y + d, ny) * NX + x} for d in order]
    rows_back = [{"tile": mod(y - d, ny) * NX + x} for d in order]
    bands_to = [{"band": mod(band + j, nb)} for j in range(nb)]

    loads = [pltpu.make_async_copy(src_hbm, src, load_sem.at[0])]
    for p, d in enumerate(order):
        loads.append(pltpu.make_async_copy(v_hbm.at[mod(y + d, ny)], v.at[p], load_sem.at[1 + p]))
    for p, d in enumerate(order):
        first = pl.multiple_of(mod(y - d, ny) * NX, NX)
        loads.append(pltpu.make_async_copy(u_hbm.at[pl.ds(first, NX)], u.at[p], load_sem.at[1 + ny + p]))
    loads.append(pltpu.make_async_copy(obs_hbm, obs, load_sem.at[1 + 2 * ny]))
    for copy in loads:
        copy.start()

    barrier = pltpu.get_barrier_semaphore()
    peers = [right, left] + rows_to[1:] + bands_to[1:]
    for peer in peers:
        pl.semaphore_signal(barrier, inc=1, device_id=peer, device_id_type=pl.DeviceIdType.MESH)

    def remote(a, b, send, recv, to):
        return pltpu.make_async_remote_copy(
            src_ref=a, dst_ref=b, send_sem=send, recv_sem=recv, device_id=to,
            device_id_type=pl.DeviceIdType.MESH)

    sent = []

    def start(copy):
        copy.start()
        sent.append(copy)

    k_index = lax.broadcasted_iota(jnp.int32, (rmax, 1), 0)

    def weight(p):
        i = mod(y + order[p], ny)
        e = vexp_ref[i] + uexp_ref[i]
        scale = jnp.where(e == 2, 4.0, jnp.where(e == 1, 2.0, jnp.where(e == 0, 1.0, jnp.where(e == -1, 0.5, 0.25))))
        return jnp.where(k_index < rank_ref[i], scale.astype(F32), 0.0)

    def y_copy(h, p):
        return remote(out.at[h, p], inc.at[h, p, x], ysend.at[h, p], yrecv.at[h, p], rows_to[p])

    def x_copy(h, p, kind):
        if kind == 0:
            block, to = inc.at[h, p, x], right
        elif kind == 1:
            block, to = inc.at[h, p, x], left
        elif p % 2 == 0:
            block, to = inc.at[h, p, xl], right
        else:
            block, to = inc.at[h, p, xr], left
        return remote(block, block, xsend.at[h, p, kind], xrecv.at[h, p, kind], to)

    def x_wait(h, p, kind):
        slot = (xl, xr, xf)[kind]
        block = inc.at[h, p, slot]
        remote(block, block, xsend.at[h, p, kind], xrecv.at[h, p, kind], right).wait_recv()

    loads[0].wait()
    groups = [[0]] + [list(range(s, min(s + 2, ny))) for s in range(1, ny, 2)]
    for n, group in enumerate(groups):
        for p in group:
            loads[1 + p].wait()
        lhs = v[group[0]:group[-1] + 1].reshape(len(group) * rmax, v.shape[2])
        result = dot(lhs, src[...])
        for q, p in enumerate(group):
            piece = (result[q * rmax:(q + 1) * rmax] * weight(p)).astype(BF16)
            for h in range(NH):
                cut = piece[:, h * width:(h + 1) * width]
                if p == 0:
                    inc[h, 0, x] = cut
                else:
                    out[h, p] = cut
        if n == 0:
            pl.semaphore_wait(barrier, len(peers))
        for h in range(NH):
            for p in group:
                if p == 0:
                    if h == 0:
                        start(x_copy(h, 0, 0))
                        start(x_copy(h, 0, 1))
                else:
                    start(y_copy(h, p))

    def arrive(h, p):
        if p > 0:
            y_copy(h, p).wait_recv()
        if p > 0 or h > 0:
            start(x_copy(h, p, 0))
            start(x_copy(h, p, 1))

    def forward(h, p):
        x_wait(h, p, p % 2)
        start(x_copy(h, p, 2))

    def turn_u(p):
        loads[1 + ny + p].wait()
        ut[p] = u[p].reshape(NX * rmax, u.shape[3]).T

    def complete(h, p):
        x_wait(h, p, 1 - p % 2)
        x_wait(h, p, 2)
        term = dot(ut[p], inc[h, p].reshape(NX * rmax, width))
        if p == 0:
            acc[h] = term
        else:
            acc[h] += term

    def ar_copy(h, j):
        return remote(ar_out.at[h, mod(band + j, nb)], ar_in.at[h, j], arsend.at[h, j], arrecv.at[h, j], bands_to[j])

    def ag_copy(h, j):
        return remote(ag_out.at[h], ag_in.at[h, band], agsend.at[h, j], agrecv.at[h, j], bands_to[j])

    def reduce_send(h):
        ar_out[h] = acc[h].reshape(nb, rb, width).astype(AR_TYPE)
        for j in range(1, nb):
            start(ar_copy(h, j))

    def reduce_sum(h):
        mine = pl.ds(pl.multiple_of(band * rb, rb), rb)
        total = acc[h, mine, :] - obs[mine, h * width:(h + 1) * width].astype(F32)
        for j in range(1, nb):
            ar_copy(h, j).wait_recv()
            total = total + ar_in[h, j].astype(F32)
        total = total.astype(AR_TYPE)
        ag_out[h] = total
        ag_in[h, band] = total
        for j in range(1, nb):
            start(ag_copy(h, j))

    def reduce_done(h):
        for j in range(1, nb):
            block = ag_in.at[h, mod(band - j, nb)]
            remote(ag_out.at[h], block, agsend.at[h, j], agrecv.at[h, j], bands_to[j]).wait_recv()
        full = ag_in[h].reshape(nb * rb, width)
        rows[h] = full.astype(BF16)

    def residual(h):
        res_t[h * width:(h + 1) * width, :] = ag_in[h].reshape(nb * rb, width).astype(F32).T

    def hop_copy(h, p):
        return remote(part.at[h, p, xf], via.at[h, p], bsend.at[h, p, 2], brecv.at[h, p, 2], right if p % 2 == 0 else left)

    def plain_copy(h, p):
        if p % 2 == 0:
            return remote(part.at[h, p, xl], from_r.at[h, p], bsend.at[h, p, 1], brecv.at[h, p, 1], left)
        return remote(part.at[h, p, xr], from_l.at[h, p], bsend.at[h, p, 0], brecv.at[h, p, 0], right)

    def comb_copy(h, p):
        if p % 2 == 0:
            return remote(comb.at[h, p], from_l.at[h, p], bsend.at[h, p, 0], brecv.at[h, p, 0], right)
        return remote(comb.at[h, p], from_r.at[h, p], bsend.at[h, p, 1], brecv.at[h, p, 1], left)

    def z_copy(h, p):
        return remote(ys.at[h, p], ret.at[h, p], zsend.at[h, p], zrecv.at[h, p], rows_back[p])

    def spread(h, p):
        term = dot(u[p].reshape(NX * rmax, u.shape[3]), rows[h])
        part[h, p] = term.astype(BF16).reshape(NX, rmax, width)
        start(hop_copy(h, p))
        start(plain_copy(h, p))

    def combine(h, p):
        hop_copy(h, p).wait_recv()
        target = xr if p % 2 == 0 else xl
        comb[h, p] = (part[h, p, target].astype(F32) + via[h, p].astype(F32)).astype(BF16)
        start(comb_copy(h, p))

    def finish(h, p):
        plain_copy(h, p).wait_recv()
        comb_copy(h, p).wait_recv()
        total = part[h, p, x].astype(F32) + from_l[h, p].astype(F32) + from_r[h, p].astype(F32)
        if p == 0:
            ret[h, 0] = total.astype(BF16)
        else:
            ys[h, p] = total.astype(BF16)
            start(z_copy(h, p))

    def gather(h, p):
        if p > 0:
            z_copy(h, p).wait_recv()
        adj[h, p * rmax:(p + 1) * rmax, :] = (ret[h, p].astype(F32) * weight(p)).astype(BF16)

    def turn_v(g):
        lo, hi = g * ny // 2, (g + 1) * ny // 2
        vt[:, lo * rmax:hi * rmax] = v[lo:hi].reshape((hi - lo) * rmax, v.shape[2]).T

    for h in range(NH):
        for p in range(ny):
            arrive(h, p)
            if h == 0:
                turn_u(p)
            if p >= LAG:
                forward(h, p - LAG)
        for p in range(ny - LAG, ny):
            forward(h, p)
        for p in range(ny):
            complete(h, p)
        if h == 0:
            loads[1 + 2 * ny].wait()
        reduce_send(h)
        if h == 0:
            turn_v(0)
        reduce_sum(h)
        if h == 0:
            turn_v(1)
        reduce_done(h)
    back = list(range(ny - 1, -1, -1))
    for h in range(NH):
        for n, p in enumerate(back):
            spread(h, p)
            if n >= LAG:
                combine(h, back[n - LAG])
        for p in back[ny - LAG:]:
            combine(h, p)
        residual(h)
        for p in back:
            finish(h, p)
    mine = pl.ds(pl.multiple_of(band * res_out.shape[0], res_out.shape[0]), res_out.shape[0])
    res_out[...] = res_t[mine, :]
    for h in range(NH):
        for p in back:
            gather(h, p)
        grad_out[:, h * width:(h + 1) * width] = dot(vt[...], adj[h]).astype(BF16)
    for copy in sent:
        copy.wait_send()


def local(sources, observed, v_factors, u_factors, tile_ranks, v_exponents, u_exponents):
    nt, nb = lax.axis_size("tile"), lax.axis_size("band")
    ny = nt // NX
    nr, rmax, b = v_factors.shape
    nrow, s = observed.shape
    width, rb = s // NH, nrow // nb
    any_space = pl.BlockSpec(memory_space=pl.ANY)
    smem = pl.BlockSpec(memory_space=pltpu.SMEM)
    vmem = pl.BlockSpec(memory_space=pltpu.VMEM)
    sem = pltpu.SemaphoreType.DMA
    res, grad = pl.pallas_call(
        functools.partial(kernel, ny, nb),
        out_shape=(
            jax.ShapeDtypeStruct((s // nb, nrow), F32),
            jax.ShapeDtypeStruct((b, s), BF16),
        ),
        in_specs=[any_space] * 4 + [smem] * 3,
        out_specs=(vmem, vmem),
        scratch_shapes=[
            pltpu.VMEM((b, s), BF16),
            pltpu.VMEM((nrow, s), BF16),
            pltpu.VMEM((ny, rmax, b), BF16),
            pltpu.VMEM((ny, NX, rmax, nrow), BF16),
            pltpu.VMEM((ny, nrow, NX * rmax), BF16),
            pltpu.VMEM((b, ny * rmax), BF16),
            pltpu.VMEM((NH, ny, NX, rmax, width), BF16),
            pltpu.VMEM((NH, ny, rmax, width), BF16),
            pltpu.VMEM((NH, nrow, width), F32),
            pltpu.VMEM((NH, nb, rb, width), AR_TYPE),
            pltpu.VMEM((NH, nb, rb, width), AR_TYPE),
            pltpu.VMEM((NH, rb, width), AR_TYPE),
            pltpu.VMEM((NH, nb, rb, width), AR_TYPE),
            pltpu.VMEM((NH, nrow, width), BF16),
            pltpu.VMEM((s, nrow), F32),
            pltpu.VMEM((NH, ny, NX, rmax, width), BF16),
        ] + [pltpu.VMEM((NH, ny, rmax, width), BF16)] * 6 + [
            pltpu.VMEM((NH, ny * rmax, width), BF16),
            sem((2 + 2 * ny,)),
            sem((NH, ny)), sem((NH, ny)),
            sem((NH, ny, 3)), sem((NH, ny, 3)),
            sem((NH, nb)), sem((NH, nb)),
            sem((NH, nb)), sem((NH, nb)),
            sem((NH, ny, 3)), sem((NH, ny, 3)),
            sem((NH, ny)), sem((NH, ny)),
        ],
        compiler_params=pltpu.CompilerParams(
            collective_id=0, has_side_effects=True, vmem_limit_bytes=48 * 1024 * 1024),
        cost_estimate=pl.CostEstimate(flops=1_600_000_000, bytes_accessed=5_000_000, transcendentals=0),
    )(sources, observed, v_factors, u_factors,
      tile_ranks.reshape(-1), v_exponents.reshape(-1), u_exponents.reshape(-1))
    return res.T, grad


def solution(mesh):
    in_specs = (
        P(("band", "tile"), None),
        P("tile", None),
        P(None, None, ("band", "tile")),
        P("band", None, "tile"),
        P(None, ("band", "tile")),
        P(None, ("band", "tile")),
        P(None, ("band", "tile")),
    )
    out_specs = (P("tile", "band"), P(("band", "tile"), None))
    return jax.shard_map(local, mesh=mesh, in_specs=in_specs, out_specs=out_specs, check_vma=False)
```

time: 239 us -> 85.2 us (0.36)
  waiting for transfers between devices: 153 us -> 0 us
  Pallas kernels: 0 us -> 74.7 us
  blocking collectives: 49.3 us -> 0 us
  between operations: 14.1 us -> 0.66 us
  starting transfers between devices: 9.89 us -> 0 us
  matrix products: 5.88 us -> 0 us
  local copies, waits for them, and re-layouts: 3.08 us -> 8.12 us
  other arithmetic: 2.71 us -> 0 us
    psum x1 -> x0, waiting for transfers between devices: 115 us -> none  [local(): totals = lax.psum(partial_value, 'band')]
    pallas_call x0 -> x1, Pallas kernels: none -> 74.7 us  [local(): pl.pallas_call(functools.partial(kernel, ny, nb), out_shape=(jax.ShapeDty...]
    all_to_all x1 -> x0, blocking collectives: 49.3 us -> none  [local(): lax.all_to_all(outgoing, 'tile', split_axis=0, concat_axis=0, tiled=True)]
    all_to_all x1 -> x0, waiting for transfers between devices: 38.7 us -> none  [local(): lax.all_to_all(adjoint_part.astype(jnp.bfloat16), 'tile', split_axis=0, c...]
    all_to_all x1 -> x0, starting transfers between devices: 9.85 us -> none  [local(): lax.all_to_all(adjoint_part.astype(jnp.bfloat16), 'tile', split_axis=0, c...]
    dot_general x4 -> x0, matrix products: 5.88 us -> none  [the longest x1 2.09 us: local(): jnp.einsum('ikb,bs->iks', v_factors, sources, preferred_element_type=jnp....]
    unnamed x8 -> x16, local copies, waits for them, and re-layouts: 2.29 us -> 8.12 us
  transfers between devices with their start and end apart: 2 -> 0, of which waited for: 2 -> 0; matrix products, arithmetic and copies ran while one was open for 0% -> 0% of each run, Pallas kernels for 0% -> 0%
where the time goes in v1:
time: 85.2 us; the launch traced here: 83.5 us
  Pallas kernels  74.7 us (88%)
  local copies, waits for them, and re-layouts  8.12 us (10%)
    pallas_call x1, Pallas kernels, local(): pl.pallas_call(functools.partial(kernel, ny, nb), out_shape=(jax.ShapeDty...  74.7 us
    unnamed x16, local copies, waits for them, and re-layouts  8.12 us

profile of v1, /device:TPU:6, one launch (start us, length us, event | category | flops | bytes accessed | tf_op | source)
XLA Modules:
  0.0 83.5 jit_solution(15287818001632113120)
XLA Ops:
  0.6 0.0 copy-start
  0.6 1.4 %copy-done = bf16[8,96,1024]{2,1,0:T(8,128)(2,1)S(1)} copy-done((bf16[8,96,1024]{2,1,0:T(8,128)(2,1)S(1)}, bf16[8,96,1024]{2,1,0:T(8,128)(2,1)}, u32[]{:S(2)}) %copy-start) | copy-done | bytes 1572888
  2.0 0.0 copy-start.1
  2.0 1.4 %copy-done.1 = bf16[32,96,256]{2,1,0:T(8,128)(2,1)S(1)} copy-done((bf16[32,96,256]{2,1,0:T(8,128)(2,1)S(1)}, bf16[32,96,256]{2,1,0:T(8,128)(2,1)}, u32[]{:S(2)}) %copy-start.1) | copy-done | bytes 1572888
  3.4 0.0 copy-start.2
  3.5 1.0 %copy-done.2 = bf16[1024,256]{1,0:T(8,128)(2,1)S(1)} copy-done((bf16[1024,256]{1,0:T(8,128)(2,1)S(1)}, bf16[1024,256]{1,0:T(8,128)(2,1)}, u32[]{:S(2)}) %copy-start.2) | copy-done | bytes 524312
  4.5 0.0 copy-start.3
  4.5 0.9 %copy-done.3 = bf16[256,256]{1,0:T(8,128)(2,1)S(1)} copy-done((bf16[256,256]{1,0:T(8,128)(2,1)S(1)}, bf16[256,256]{1,0:T(8,128)(2,1)}, u32[]{:S(2)}) %copy-start.3) | copy-done | bytes 131096
  5.4 0.0 copy-start.4
  5.4 0.7 copy-done.4
  6.1 0.0 copy-start.5
  6.1 0.7 copy-done.5
  6.7 0.0 copy-start.6
  6.7 0.7 copy-done.6
  7.4 74.7 %shard_map.86 = (f32[16,256]{1,0:T(8,128)S(1)}, bf16[1024,256]{1,0:T(8,128)(2,1)S(1)}) custom-call(bf16[1024,256]{1,0:T(8,128)(2,1)S(1)} %copy-done.2, bf16[256,256]{1,0:T(8,128)(2,1)S(1)} %copy-done.3, bf16[8,96,1024]{2,1,0:T(8,128)(2,1)S(1)} %copy-done, bf16[32,96,256]{2,1,0:T(8,128)(2,1)S(1)} %copy-done.1, s32[8]{0:T(128)S(1)} %bitcast.5, s32[8]{0:T(128)S(1)} %bitcast.6, ...), custom_call_target="tpu_custom_call" | custom-call | flops 1600000000 | bytes 5000000 | tf_op jit(solution)/shard_map/pallas_call | solution.py:290
  82.1 0.6 copy.11
  82.7 0.8 copy.12
Async XLA Ops:
  0.6 1.4 %copy-start = (bf16[8,96,1024]{2,1,0:T(8,128)(2,1)S(1)}, bf16[8,96,1024]{2,1,0:T(8,128)(2,1)}, u32[]{:S(2)}) copy-start(bf16[8,96,1024]{2,1,0:T(8,128)(2,1)} %v_hbm.1) | copy-start | bytes 4718596
  2.0 1.4 %copy-start.1 = (bf16[32,96,256]{2,1,0:T(8,128)(2,1)S(1)}, bf16[32,96,256]{2,1,0:T(8,128)(2,1)}, u32[]{:S(2)}) copy-start(bf16[32,96,256]{2,1,0:T(8,128)(2,1)} %u_hbm.1) | copy-start | bytes 4718596
  3.4 1.0 %copy-start.2 = (bf16[1024,256]{1,0:T(8,128)(2,1)S(1)}, bf16[1024,256]{1,0:T(8,128)(2,1)}, u32[]{:S(2)}) copy-start(bf16[1024,256]{1,0:T(8,128)(2,1)} %src_hbm.1) | copy-start | bytes 1572868
  4.5 0.9 %copy-start.3 = (bf16[256,256]{1,0:T(8,128)(2,1)S(1)}, bf16[256,256]{1,0:T(8,128)(2,1)}, u32[]{:S(2)}) copy-start(bf16[256,256]{1,0:T(8,128)(2,1)} %obs_hbm.1) | copy-start | bytes 393220
  5.4 0.7 copy-start.4
  6.1 0.7 copy-start.5
  6.7 0.7 copy-start.6

commit v2 on v0

v2 whole, which is shorter than its diff:
```python
import functools

import jax
import jax.numpy as jnp
from jax import lax
from jax.experimental import pallas as pl
from jax.experimental.pallas import tpu as pltpu
from jax.sharding import PartitionSpec as P

NX = 4
NH = 2
F32, BF16 = jnp.float32, jnp.bfloat16
AR_TYPE = jnp.bfloat16


def displacements(ny):
    order, groups = [0], [[0]]
    for step in range(1, ny // 2 + 1):
        group = [step] if ny - step == step else [step, ny - step]
        groups.append(list(range(len(order), len(order) + len(group))))
        order += group
    return order, groups


def dot(a, b):
    return jnp.dot(a, b, preferred_element_type=F32)


def kernel(
    ny, nb,
    src_hbm, obs_hbm, v_hbm, u_hbm, rank_hbm, vexp_hbm, uexp_hbm,
    res_out, adj_out,
    rank_ref, vexp_ref, uexp_ref, src, obs, v, u, ut, inc, out, acc,
    ar_out, ar_in, ag_out, ag_in, rows, res_t,
    part, via, comb, from_l, from_r, ys, ret,
    load_sem, v_sem, u_sem, ysend, yrecv, xsend, xown, xfwd, arsend, arrecv, agsend, agrecv,
    bsend, bhop, brest, zsend, zrecv,
):
    tile = lax.axis_index("tile")
    band = lax.axis_index("band")
    y, x = tile // NX, tile % NX
    order, groups = displacements(ny)
    ng = len(groups)
    rmax = v.shape[1]
    width = inc.shape[-1]
    rb = ar_out.shape[2]
    nrow = u.shape[3]

    def mod(value, n):
        return lax.rem(value + n, n)

    xr, xl, xf = mod(x + 1, NX), mod(x - 1, NX), mod(x + 2, NX)
    right, left = {"tile": y * NX + xr}, {"tile": y * NX + xl}
    rows_to = [{"tile": mod(y + d, ny) * NX + x} for d in order]
    rows_back = [{"tile": mod(y - d, ny) * NX + x} for d in order]
    bands_to = [{"band": mod(band + j, nb)} for j in range(nb)]
    band_order = sorted(range(1, nb), key=lambda j: -min(j, nb - j))

    barrier = pltpu.get_barrier_semaphore()
    peers = [right, left] + rows_to[1:] + bands_to[1:]
    for peer in peers:
        pl.semaphore_signal(barrier, inc=1, device_id=peer, device_id_type=pl.DeviceIdType.MESH)

    v_groups = [[0, 1, 2], [5, 6, 7], [3, 4]] if ny == 8 else groups

    def v_copy(p):
        n = [p in group for group in v_groups].index(True)
        return pltpu.make_async_copy(v_hbm.at[mod(y + order[p], ny)], v.at[p], v_sem.at[n])

    def u_copy(g, p):
        first = pl.multiple_of(mod(y - order[p], ny) * NX, NX)
        return pltpu.make_async_copy(u_hbm.at[pl.ds(first, NX)], u.at[:, p], u_sem.at[g])

    small = [
        pltpu.make_async_copy(a, b, load_sem.at[n])
        for n, (a, b) in enumerate(((rank_hbm, rank_ref), (vexp_hbm, vexp_ref), (uexp_hbm, uexp_ref)))
    ]
    load_src = pltpu.make_async_copy(src_hbm, src, load_sem.at[3])
    load_obs = pltpu.make_async_copy(obs_hbm, obs, load_sem.at[4])
    load_src.start()
    for p in v_groups[0]:
        v_copy(p).start()
    for copy in small:
        copy.start()
    for group in v_groups[1:]:
        for p in group:
            v_copy(p).start()
    for g in range(ng):
        for p in groups[g]:
            u_copy(g, p).start()
    load_obs.start()

    def remote(a, b, send, recv, to):
        return pltpu.make_async_remote_copy(
            src_ref=a, dst_ref=b, send_sem=send, recv_sem=recv, device_id=to,
            device_id_type=pl.DeviceIdType.MESH)

    def arrived(ref, send, recv):
        remote(ref, ref, send, recv, right).wait_recv()

    def left_here(ref, send, recv):
        remote(ref, ref, send, recv, right).wait_send()

    k_index = lax.broadcasted_iota(jnp.int32, (rmax, 1), 0)

    def weight(p):
        i = mod(y + order[p], ny)
        e = vexp_ref[i] + uexp_ref[i]
        scale = jnp.where(e == 2, 4.0, jnp.where(e == 1, 2.0, jnp.where(e == 0, 1.0, jnp.where(e == -1, 0.5, 0.25))))
        return jnp.where(k_index < rank_ref[i], scale.astype(F32), 0.0)

    def span(g):
        return slice(groups[g][0], groups[g][-1] + 1)

    def group_of(p):
        return [p in group for group in groups].index(True)

    def y_start(h, p):
        remote(out.at[h, p - 1], inc.at[h, x, p], ysend.at[0], yrecv.at[h, group_of(p)], rows_to[p]).start()

    def own_start(h, g):
        block = inc.at[h, x, span(g)]
        remote(block, block, xsend.at[0], xown.at[h, g], right).start()
        remote(block, block, xsend.at[0], xown.at[h, g], left).start()

    load_src.wait()
    for n, group in enumerate(v_groups):
        cut = slice(group[0], group[-1] + 1)
        pltpu.make_async_copy(v.at[cut], v.at[cut], v_sem.at[n]).wait()
        result = dot(v[cut].reshape(len(group) * rmax, v.shape[2]), src[...])
        if n == 0:
            for copy in small:
                copy.wait()
        for q, p in enumerate(group):
            piece = (result[q * rmax:(q + 1) * rmax] * weight(p)).astype(BF16)
            for h in range(NH):
                half = piece[:, h * width:(h + 1) * width]
                if p == 0:
                    inc[h, x, 0] = half
                else:
                    out[h, p - 1] = half
        if n == 0:
            pl.semaphore_wait(barrier, len(peers))
            own_start(0, 0)
            own_start(1, 0)
        for p in group:
            if p > 0:
                y_start(0, p)

    def arrive(h, g):
        if g > 0:
            arrived(inc.at[h, 0, span(g)], ysend.at[0], yrecv.at[h, g])
        if g > 0:
            own_start(h, g)
        if h + 1 < NH:
            for p in groups[g]:
                if p > 0:
                    y_start(h + 1, p)

    def forward(h, g):
        arrived(inc.at[h, 0:2, span(g)], xsend.at[0], xown.at[h, g])
        for p in groups[g]:
            block = inc.at[h, xl if p % 2 == 0 else xr, p]
            remote(block, block, xsend.at[0], xfwd.at[h, g], right if p % 2 == 0 else left).start()

    def k_span(g):
        return slice(groups[g][0] * NX * rmax, (groups[g][-1] + 1) * NX * rmax)

    def turn_u(g):
        block = u.at[:, span(g)]
        pltpu.make_async_copy(block, block, u_sem.at[g]).wait()
        ut[:, k_span(g)] = u[:, span(g)].reshape(-1, nrow).T

    def complete(h, g):
        arrived(inc.at[h, 0, span(g)], xsend.at[0], xfwd.at[h, g])
        term = dot(ut[:, k_span(g)], inc[h, :, span(g)].reshape(-1, width))
        if g == 0:
            acc[h] = term
        else:
            acc[h] += term

    def reduce_send(h):
        ar_out[h] = acc[h].reshape(nb, rb, width).astype(AR_TYPE)
        for j in band_order:
            remote(ar_out.at[h, mod(band + j, nb)], ar_in.at[h, j], arsend.at[0], arrecv.at[h], bands_to[j]).start()

    def reduce_sum(h):
        mine = pl.ds(pl.multiple_of(band * rb, rb), rb)
        total = acc[h, mine, :] - obs[mine, h * width:(h + 1) * width].astype(F32)
        arrived(ar_in.at[h, 1:nb], arsend.at[0], arrecv.at[h])
        for j in range(1, nb):
            total = total + ar_in[h, j].astype(F32)
        total = total.astype(AR_TYPE)
        ag_out[h] = total
        ag_in[h, band] = total
        for j in band_order:
            remote(ag_out.at[h], ag_in.at[h, band], agsend.at[0], agrecv.at[h], bands_to[j]).start()

    def reduce_done(h):
        arrived(ar_in.at[h, 1:nb], agsend.at[0], agrecv.at[h])
        rows[h] = ag_in[h].reshape(nb * rb, width).astype(BF16)

    def residual(h):
        res_t[h * width:(h + 1) * width, :] = ag_in[h].reshape(nb * rb, width).astype(F32).T

    def hop_start(h, p):
        remote(part.at[h, xf, p], via.at[h, p], bsend.at[0], bhop.at[h, group_of(p)],
               right if p % 2 == 0 else left).start()

    def plain_start(h, p):
        if p % 2 == 0:
            remote(part.at[h, xl, p], from_r.at[h, p], bsend.at[0], brest.at[h, group_of(p)], left).start()
        else:
            remote(part.at[h, xr, p], from_l.at[h, p], bsend.at[0], brest.at[h, group_of(p)], right).start()

    def spread(h, g):
        term = dot(u[:, span(g)].reshape(-1, nrow), rows[h])
        part[h, :, span(g)] = term.astype(BF16).reshape(NX, len(groups[g]), rmax, width)
        for p in groups[g]:
            hop_start(h, p)

    def combine(h, g):
        arrived(via.at[h, span(g)], bsend.at[0], bhop.at[h, g])
        for p in groups[g]:
            target = xr if p % 2 == 0 else xl
            comb[h, p] = (part[h, target, p].astype(F32) + via[h, p].astype(F32)).astype(BF16)
            remote(comb.at[h, p], (from_l if p % 2 == 0 else from_r).at[h, p], bsend.at[0], brest.at[h, g],
                   right if p % 2 == 0 else left).start()

    def finish(h, g):
        arrived(part.at[h, 0:2, span(g)], bsend.at[0], brest.at[h, g])
        for p in groups[g]:
            total = part[h, x, p].astype(F32) + from_l[h, p].astype(F32) + from_r[h, p].astype(F32)
            if p == 0:
                ret[h, 0] = total.astype(BF16)
            else:
                ys[h, p - 1] = total.astype(BF16)
                remote(ys.at[h, p - 1], ret.at[h, p], zsend.at[0], zrecv.at[h, g], rows_back[p]).start()

    def gather(h, g):
        if g > 0:
            arrived(ret.at[h, span(g)], zsend.at[0], zrecv.at[h, g])
        for p in groups[g]:
            adj_out[mod(y + order[p], ny), :, h * width:(h + 1) * width] = (
                ret[h, p].astype(F32) * weight(p)).astype(BF16)

    back = list(range(ng - 1, -1, -1))

    def spread_all(h):
        for n, g in enumerate(back):
            spread(h, g)
            if n > 0:
                for p in groups[back[n - 1]]:
                    plain_start(h, p)
        for p in groups[back[-1]]:
            plain_start(h, p)

    arrive(0, 0)
    arrive(0, 1)
    turn_u(0)
    turn_u(1)
    arrive(0, 2)
    forward(0, 0)
    turn_u(2)
    arrive(0, 3)
    forward(0, 1)
    arrive(0, 4)
    turn_u(3)
    turn_u(4)
    forward(0, 2)
    arrive(1, 1)
    forward(0, 3)
    arrive(1, 2)
    complete(0, 0)
    complete(0, 1)
    forward(0, 4)
    arrive(1, 3)
    complete(0, 2)
    complete(0, 3)
    arrive(1, 4)
    complete(0, 4)
    load_obs.wait()
    reduce_send(0)
    forward(1, 0)
    forward(1, 1)
    forward(1, 2)
    forward(1, 3)
    forward(1, 4)
    complete(1, 0)
    complete(1, 1)
    complete(1, 2)
    complete(1, 3)
    reduce_sum(0)
    complete(1, 4)
    reduce_send(1)
    reduce_sum(1)
    reduce_done(0)
    spread_all(0)
    residual(0)
    for g in back:
        combine(0, g)
    reduce_done(1)
    spread_all(1)
    for g in back:
        finish(0, g)
    for g in back:
        combine(1, g)
    residual(1)
    mine = pl.ds(pl.multiple_of(band * res_out.shape[0], res_out.shape[0]), res_out.shape[0])
    res_out[...] = res_t[mine, :]
    for g in back:
        gather(0, g)
    for g in back:
        finish(1, g)
    for g in back:
        gather(1, g)
    left_here(out, ysend.at[0], yrecv.at[0, 0])
    left_here(inc.at[:, 0:3], xsend.at[0], xown.at[0, 0])
    left_here(ar_in.at[:, 1:nb], arsend.at[0], arrecv.at[0])
    left_here(ar_in.at[:, 1:nb], agsend.at[0], agrecv.at[0])
    left_here(part.at[:, 0:3], bsend.at[0], bhop.at[0, 0])
    left_here(ys, zsend.at[0], zrecv.at[0, 0])


def last_kernel(v, adj, res, grad_out, res_out):
    k = v.shape[0] * v.shape[1]
    grad_out[...] = lax.dot_general(
        v[...].reshape(k, v.shape[2]), adj[...].reshape(k, adj.shape[2]), (((0,), (0,)), ((), ())),
        preferred_element_type=F32).astype(BF16)
    res_out[...] = res[...]


def local(sources, observed, v_factors, u_factors, tile_ranks, v_exponents, u_exponents):
    nt, nb = lax.axis_size("tile"), lax.axis_size("band")
    ny = nt // NX
    nr, rmax, b = v_factors.shape
    nrow, s = observed.shape
    width, rb = s // NH, nrow // nb
    ng = len(displacements(ny)[1])
    hbm = pl.BlockSpec(memory_space=pl.ANY)
    vmem = pl.BlockSpec(memory_space=pltpu.VMEM)
    sem = pltpu.SemaphoreType.DMA
    res, adj = pl.pallas_call(
        functools.partial(kernel, ny, nb),
        out_shape=(
            jax.ShapeDtypeStruct((s // nb, nrow), F32),
            jax.ShapeDtypeStruct((nr, rmax, s), BF16),
        ),
        in_specs=[hbm] * 7,
        out_specs=(vmem, vmem),
        scratch_shapes=[
            pltpu.SMEM((nr,), jnp.int32),
            pltpu.SMEM((nr,), jnp.int32),
            pltpu.SMEM((nr,), jnp.int32),
            pltpu.VMEM((b, s), BF16),
            pltpu.VMEM((nrow, s), BF16),
            pltpu.VMEM((ny, rmax, b), BF16),
            pltpu.VMEM((NX, ny, rmax, nrow), BF16),
            pltpu.VMEM((nrow, ny * NX * rmax), BF16),
            pltpu.VMEM((NH, NX, ny, rmax, width), BF16),
            pltpu.VMEM((NH, ny - 1, rmax, width), BF16),
            pltpu.VMEM((NH, nrow, width), F32),
            pltpu.VMEM((NH, nb, rb, width), AR_TYPE),
            pltpu.VMEM((NH, nb, rb, width), AR_TYPE),
            pltpu.VMEM((NH, rb, width), AR_TYPE),
            pltpu.VMEM((NH, nb, rb, width), AR_TYPE),
            pltpu.VMEM((NH, nrow, width), BF16),
            pltpu.VMEM((s, nrow), F32),
            pltpu.VMEM((NH, NX, ny, rmax, width), BF16),
            pltpu.VMEM((NH, ny, rmax, width), BF16),
            pltpu.VMEM((NH, ny, rmax, width), BF16),
            pltpu.VMEM((NH, ny, rmax, width), BF16),
            pltpu.VMEM((NH, ny, rmax, width), BF16),
            pltpu.VMEM((NH, ny - 1, rmax, width), BF16),
            pltpu.VMEM((NH, ny, rmax, width), BF16),
            sem((5,)), sem((ng,)), sem((ng,)),
            sem((1,)), sem((NH, ng)),
            sem((1,)), sem((NH, ng)), sem((NH, ng)),
            sem((1,)), sem((NH,)),
            sem((1,)), sem((NH,)),
            sem((1,)), sem((NH, ng)), sem((NH, ng)),
            sem((1,)), sem((NH, ng)),
        ],
        compiler_params=pltpu.CompilerParams(
            collective_id=0, has_side_effects=True, vmem_limit_bytes=60 * 1024 * 1024),
        cost_estimate=pl.CostEstimate(flops=1_600_000_000, bytes_accessed=5_000_000, transcendentals=0),
    )(sources, observed, v_factors, u_factors,
      tile_ranks.reshape(-1), v_exponents.reshape(-1), u_exponents.reshape(-1))
    steps = 4
    grad, res = pl.pallas_call(
        last_kernel,
        grid=(steps,),
        out_shape=(jax.ShapeDtypeStruct((b, s), BF16), jax.ShapeDtypeStruct(res.shape, F32)),
        in_specs=[
            pl.BlockSpec((nr, rmax, b // steps), lambda i: (0, 0, i)),
            pl.BlockSpec(adj.shape, lambda i: (0, 0, 0)),
            pl.BlockSpec(res.shape, lambda i: (0, 0)),
        ],
        out_specs=(
            pl.BlockSpec((b // steps, s), lambda i: (i, 0)),
            pl.BlockSpec(res.shape, lambda i: (0, 0)),
        ),
        compiler_params=pltpu.CompilerParams(vmem_limit_bytes=62 * 1024 * 1024),
    )(v_factors, adj, res)
    return res.T, grad


def solution(mesh):
    in_specs = (
        P(("band", "tile"), None),
        P("tile", None),
        P(None, None, ("band", "tile")),
        P("band", None, "tile"),
        P(None, ("band", "tile")),
        P(None, ("band", "tile")),
        P(None, ("band", "tile")),
    )
    out_specs = (P("tile", "band"), P(("band", "tile"), None))
    return jax.shard_map(local, mesh=mesh, in_specs=in_specs, out_specs=out_specs, check_vma=False)
```

time: 239 us -> 70.2 us (0.29)
  the two profiles are of different devices: /device:TPU:6 before, /device:TPU:8 now
where the time goes in v2:
time: 70.2 us; the launch traced here: 70 us
  Pallas kernels  69.4 us (99%)
    pallas_call x1, Pallas kernels, local(): pl.pallas_call(functools.partial(kernel, ny, nb), out_shape=(jax.ShapeDty...  65.3 us
    pallas_call x1, Pallas kernels, local(): pl.pallas_call(last_kernel, grid=(steps,), out_shape=(jax.ShapeDtypeStruc...  4.1 us

profile of v2, /device:TPU:8, one launch (start us, length us, event | category | flops | bytes accessed | tf_op | source)
XLA Modules:
  0.0 70.0 jit_solution(594313515189251823)
XLA Ops:
  0.6 65.3 %shard_map.86 = (f32[16,256]{1,0:T(8,128)}, bf16[8,96,256]{2,1,0:T(8,128)(2,1)}) custom-call(bf16[1024,256]{1,0:T(8,128)(2,1)} %src_hbm.1, bf16[256,256]{1,0:T(8,128)(2,1)} %obs_hbm.1, bf16[8,96,1024]{2,1,0:T(8,128)(2,1)} %v.1, bf16[32,96,256]{2,1,0:T(8,128)(2,1)} %u_hbm.1, s32[8]{0:T(128)} %bitcast.5, s32[8]{0:T(128)} %bitcast.6, s32[8]{0:T(128)} %bitcast.7), custom_call_target="tpu_custom_call" | custom-call | flops 1600000000 | bytes 5000000 | tf_op jit(solution)/shard_map/pallas_call | solution.py:343
  65.9 4.1 %shard_map.87 = (bf16[1024,256]{1,0:T(8,128)(2,1)}, f32[16,256]{1,0:T(8,128)}) custom-call(bf16[8,96,1024]{2,1,0:T(8,128)(2,1)} %v.1, bf16[8,96,256]{2,1,0:T(8,128)(2,1)} %get-tuple-element.6.adj, f32[16,256]{1,0:T(8,128)} %get-tuple-element.7.res), custom_call_target="tpu_custom_call" | custom-call | tf_op jit(solution)/shard_map/pallas_call | solution.py:390

commit v3 on v2

--- a/solution.py
+++ b/solution.py
@@ -56,11 +56,6 @@
     bands_to = [{"band": mod(band + j, nb)} for j in range(nb)]
     band_order = sorted(range(1, nb), key=lambda j: -min(j, nb - j))
 
-    barrier = pltpu.get_barrier_semaphore()
-    peers = [right, left] + rows_to[1:] + bands_to[1:]
-    for peer in peers:
-        pl.semaphore_signal(barrier, inc=1, device_id=peer, device_id_type=pl.DeviceIdType.MESH)
-
     v_groups = [[0, 1, 2], [5, 6, 7], [3, 4]] if ny == 8 else groups
 
     def v_copy(p):
@@ -82,6 +77,12 @@
         v_copy(p).start()
     for copy in small:
         copy.start()
+
+    barrier = pltpu.get_barrier_semaphore()
+    peers = [right, left] + rows_to[1:] + bands_to[1:]
+    for peer in peers:
+        pl.semaphore_signal(barrier, inc=1, device_id=peer, device_id_type=pl.DeviceIdType.MESH)
+
     for group in v_groups[1:]:
         for p in group:
             v_copy(p).start()
@@ -249,11 +250,9 @@
     def spread_all(h):
         for n, g in enumerate(back):
             spread(h, g)
-            if n > 0:
-                for p in groups[back[n - 1]]:
-                    plain_start(h, p)
-        for p in groups[back[-1]]:
-            plain_start(h, p)
+        for g in back:
+            for p in groups[g]:
+                plain_start(h, p)
 
     arrive(0, 0)
     arrive(0, 1)
@@ -267,17 +266,17 @@
     arrive(0, 4)
     turn_u(3)
     turn_u(4)
+    arrive(1, 1)
     forward(0, 2)
-    arrive(1, 1)
+    arrive(1, 2)
     forward(0, 3)
-    arrive(1, 2)
     complete(0, 0)
+    forward(0, 4)
     complete(0, 1)
-    forward(0, 4)
     arrive(1, 3)
     complete(0, 2)
+    arrive(1, 4)
     complete(0, 3)
-    arrive(1, 4)
     complete(0, 4)
     load_obs.wait()
     reduce_send(0)
@@ -293,9 +292,9 @@
     reduce_sum(0)
     complete(1, 4)
     reduce_send(1)
-    reduce_sum(1)
     reduce_done(0)
     spread_all(0)
+    reduce_sum(1)
     residual(0)
     for g in back:
         combine(0, g)
@@ -386,7 +385,7 @@
         cost_estimate=pl.CostEstimate(flops=1_600_000_000, bytes_accessed=5_000_000, transcendentals=0),
     )(sources, observed, v_factors, u_factors,
       tile_ranks.reshape(-1), v_exponents.reshape(-1), u_exponents.reshape(-1))
-    steps = 4
+    steps = 2
     grad, res = pl.pallas_call(
         last_kernel,
         grid=(steps,),

time: 70.2 us -> 67 us (0.954)
  the two profiles are of different devices: /device:TPU:8 before, /device:TPU:6 now
where the time goes in v3:
time: 67 us; the launch traced here: 66.2 us
  Pallas kernels  65.6 us (98%)
    pallas_call x1, Pallas kernels, local(): pl.pallas_call(functools.partial(kernel, ny, nb), out_shape=(jax.ShapeDty...  62.8 us
    pallas_call x1, Pallas kernels, local(): pl.pallas_call(last_kernel, grid=(steps,), out_shape=(jax.ShapeDtypeStruc...  2.81 us

profile of v3, /device:TPU:6, one launch (start us, length us, event | category | flops | bytes accessed | tf_op | source)
XLA Modules:
  0.0 66.2 jit_solution(5456438836828275822)
XLA Ops:
  0.6 62.8 %shard_map.86 = (f32[16,256]{1,0:T(8,128)}, bf16[8,96,256]{2,1,0:T(8,128)(2,1)}) custom-call(bf16[1024,256]{1,0:T(8,128)(2,1)} %src_hbm.1, bf16[256,256]{1,0:T(8,128)(2,1)} %obs_hbm.1, bf16[8,96,1024]{2,1,0:T(8,128)(2,1)} %v.1, bf16[32,96,256]{2,1,0:T(8,128)(2,1)} %u_hbm.1, s32[8]{0:T(128)} %bitcast.5, s32[8]{0:T(128)} %bitcast.6, s32[8]{0:T(128)} %bitcast.7), custom_call_target="tpu_custom_call" | custom-call | flops 1600000000 | bytes 5000000 | tf_op jit(solution)/shard_map/pallas_call | solution.py:342
  63.4 2.8 %shard_map.87 = (bf16[1024,256]{1,0:T(8,128)(2,1)}, f32[16,256]{1,0:T(8,128)}) custom-call(bf16[8,96,1024]{2,1,0:T(8,128)(2,1)} %v.1, bf16[8,96,256]{2,1,0:T(8,128)(2,1)} %get-tuple-element.6.adj, f32[16,256]{1,0:T(8,128)} %get-tuple-element.7.res), custom_call_target="tpu_custom_call" | custom-call | tf_op jit(solution)/shard_map/pallas_call | solution.py:389

commit v4 on v3

--- a/solution.py
+++ b/solution.py
@@ -51,6 +51,7 @@
 
     xr, xl, xf = mod(x + 1, NX), mod(x - 1, NX), mod(x + 2, NX)
     right, left = {"tile": y * NX + xr}, {"tile": y * NX + xl}
+    across = {"tile": y * NX + xf}
     rows_to = [{"tile": mod(y + d, ny) * NX + x} for d in order]
     rows_back = [{"tile": mod(y - d, ny) * NX + x} for d in order]
     bands_to = [{"band": mod(band + j, nb)} for j in range(nb)]
@@ -79,17 +80,13 @@
         copy.start()
 
     barrier = pltpu.get_barrier_semaphore()
-    peers = [right, left] + rows_to[1:] + bands_to[1:]
+    peers = [right, left, across] + rows_to[1:] + bands_to[1:]
     for peer in peers:
         pl.semaphore_signal(barrier, inc=1, device_id=peer, device_id_type=pl.DeviceIdType.MESH)
 
     for group in v_groups[1:]:
         for p in group:
             v_copy(p).start()
-    for g in range(ng):
-        for p in groups[g]:
-            u_copy(g, p).start()
-    load_obs.start()
 
     def remote(a, b, send, recv, to):
         return pltpu.make_async_remote_copy(
@@ -123,6 +120,8 @@
         block = inc.at[h, x, span(g)]
         remote(block, block, xsend.at[0], xown.at[h, g], right).start()
         remote(block, block, xsend.at[0], xown.at[h, g], left).start()
+        if h == 0 and g == ng - 1:
+            remote(block, block, xsend.at[0], xfwd.at[h, g], across).start()
 
     load_src.wait()
     for n, group in enumerate(v_groups):
@@ -148,6 +147,11 @@
             if p > 0:
                 y_start(0, p)
 
+    for g in range(ng):
+        for p in groups[g]:
+            u_copy(g, p).start()
+    load_obs.start()
+
     def arrive(h, g):
         if g > 0:
             arrived(inc.at[h, 0, span(g)], ysend.at[0], yrecv.at[h, g])
@@ -159,6 +163,9 @@
                     y_start(h + 1, p)
 
     def forward(h, g):
+        if h == 0 and g == ng - 1:
+            arrived(inc.at[h, 0:2, span(g)], xsend.at[0], xown.at[h, g])
+            return
         arrived(inc.at[h, 0:2, span(g)], xsend.at[0], xown.at[h, g])
         for p in groups[g]:
             block = inc.at[h, xl if p % 2 == 0 else xr, p]
@@ -236,11 +243,11 @@
                 ret[h, 0] = total.astype(BF16)
             else:
                 ys[h, p - 1] = total.astype(BF16)
-                remote(ys.at[h, p - 1], ret.at[h, p], zsend.at[0], zrecv.at[h, g], rows_back[p]).start()
+                remote(ys.at[h, p - 1], ret.at[h, p], zsend.at[0], zrecv.at[h], rows_back[p]).start()
 
     def gather(h, g):
-        if g > 0:
-            arrived(ret.at[h, span(g)], zsend.at[0], zrecv.at[h, g])
+        if g == ng - 1:
+            arrived(ret.at[h, 1:ny], zsend.at[0], zrecv.at[h])
         for p in groups[g]:
             adj_out[mod(y + order[p], ny), :, h * width:(h + 1) * width] = (
                 ret[h, p].astype(F32) * weight(p)).astype(BF16)
@@ -293,24 +300,39 @@
     complete(1, 4)
     reduce_send(1)
     reduce_done(0)
-    spread_all(0)
+    for g in back[:2]:
+        spread(0, g)
     reduce_sum(1)
+    for g in back[2:]:
+        spread(0, g)
+    for g in back:
+        for p in groups[g]:
+            plain_start(0, p)
     residual(0)
     for g in back:
         combine(0, g)
     reduce_done(1)
-    spread_all(1)
+    for g in back:
+        spread(1, g)
+    for g in back[:2]:
+        for p in groups[g]:
+            plain_start(1, p)
     for g in back:
         finish(0, g)
-    for g in back:
+    for g in back[:2]:
+        combine(1, g)
+    for g in back[2:]:
+        for p in groups[g]:
+            plain_start(1, p)
+    for g in back[2:]:
         combine(1, g)
     residual(1)
     mine = pl.ds(pl.multiple_of(band * res_out.shape[0], res_out.shape[0]), res_out.shape[0])
     res_out[...] = res_t[mine, :]
     for g in back:
+        finish(1, g)
+    for g in back:
         gather(0, g)
-    for g in back:
-        finish(1, g)
     for g in back:
         gather(1, g)
     left_here(out, ysend.at[0], yrecv.at[0, 0])
@@ -318,7 +340,7 @@
     left_here(ar_in.at[:, 1:nb], arsend.at[0], arrecv.at[0])
     left_here(ar_in.at[:, 1:nb], agsend.at[0], agrecv.at[0])
     left_here(part.at[:, 0:3], bsend.at[0], bhop.at[0, 0])
-    left_here(ys, zsend.at[0], zrecv.at[0, 0])
+    left_here(ys, zsend.at[0], zrecv.at[0])
 
 
 def last_kernel(v, adj, res, grad_out, res_out):
@@ -372,13 +394,13 @@
             pltpu.VMEM((NH, ny, rmax, width), BF16),
             pltpu.VMEM((NH, ny - 1, rmax, width), BF16),
             pltpu.VMEM((NH, ny, rmax, width), BF16),
-            sem((5,)), sem((ng,)), sem((ng,)),
+            sem((5,)), sem((len(displacements(ny)[1]),)), sem((ng,)),
             sem((1,)), sem((NH, ng)),
             sem((1,)), sem((NH, ng)), sem((NH, ng)),
             sem((1,)), sem((NH,)),
             sem((1,)), sem((NH,)),
             sem((1,)), sem((NH, ng)), sem((NH, ng)),
-            sem((1,)), sem((NH, ng)),
+            sem((1,)), sem((NH,)),
         ],
         compiler_params=pltpu.CompilerParams(
             collective_id=0, has_side_effects=True, vmem_limit_bytes=60 * 1024 * 1024),

time: 67 us -> 65.9 us (0.984)
  Pallas kernels: 65.6 us -> 64.8 us
    pallas_call x1, Pallas kernels: 62.8 us -> 62 us  [local(): pl.pallas_call(functools.partial(kernel, ny, nb), out_shape=(jax.ShapeDty...]
where the time goes in v4:
time: 65.9 us; the launch traced here: 65.4 us
  Pallas kernels  64.8 us (98%)
    pallas_call x1, Pallas kernels, local(): pl.pallas_call(functools.partial(kernel, ny, nb), out_shape=(jax.ShapeDty...  62 us
    pallas_call x1, Pallas kernels, local(): pl.pallas_call(last_kernel, grid=(steps,), out_shape=(jax.ShapeDtypeStruc...  2.81 us

profile of v4, /device:TPU:6, one launch (start us, length us, event | category | flops | bytes accessed | tf_op | source)
XLA Modules:
  0.0 65.4 jit_solution(6999057767468123952)
XLA Ops:
  0.6 62.0 %shard_map.86 = (f32[16,256]{1,0:T(8,128)}, bf16[8,96,256]{2,1,0:T(8,128)(2,1)}) custom-call(bf16[1024,256]{1,0:T(8,128)(2,1)} %src_hbm.1, bf16[256,256]{1,0:T(8,128)(2,1)} %obs_hbm.1, bf16[8,96,1024]{2,1,0:T(8,128)(2,1)} %v.1, bf16[32,96,256]{2,1,0:T(8,128)(2,1)} %u_hbm.1, s32[8]{0:T(128)} %bitcast.5, s32[8]{0:T(128)} %bitcast.6, s32[8]{0:T(128)} %bitcast.7), custom_call_target="tpu_custom_call" | custom-call | flops 1600000000 | bytes 5000000 | tf_op jit(solution)/shard_map/pallas_call | solution.py:364
  62.6 2.8 %shard_map.87 = (bf16[1024,256]{1,0:T(8,128)(2,1)}, f32[16,256]{1,0:T(8,128)}) custom-call(bf16[8,96,1024]{2,1,0:T(8,128)(2,1)} %v.1, bf16[8,96,256]{2,1,0:T(8,128)(2,1)} %get-tuple-element.6.adj, f32[16,256]{1,0:T(8,128)} %get-tuple-element.7.res), custom_call_target="tpu_custom_call" | custom-call | tf_op jit(solution)/shard_map/pallas_call | solution.py:411
